TPU v7x, 512 devices: a whole 4x4x16 slice. The times are simulated.
512 devices in a mesh: ctx: 16 (over y, x), tp: 8 (over z_lo, core), dp: 4 (over z_hi).
Axes of the slice: x: 4, y: 4, z: 16 (z_hi: 4, z_lo: 4; z = z_hi * 4 + z_lo), core: 2. Of those that a mesh axis runs over, the one named last changes fastest.
Arguments:
- queries: bfloat16 [8192, 8192], P(('dp', 'ctx'), 'tp'), parts along dimension 0
- key_rows: bfloat16 [8192, 1024], P(('dp', 'ctx'), 'tp'), parts along dimension 0
- value_rows: bfloat16 [8192, 1024], P(('dp', 'ctx'), 'tp'), parts along dimension 0, may hold values from -6 to 6
- doc_lengths: int32 [32], P('dp'), parts along dimension 0, may hold values from 1 to 1024, 2048 in all
- unit_source: int32 [1024], P('dp'), parts along dimension 0, may hold values from 0 to 255, as said below
- w_out: bfloat16 [8192, 16384], P('tp', 'ctx'), may hold values from -0.0625 to 0.0625
Outputs:
- projected: bfloat16 [8192, 16384], P(('dp', 'tp'), 'ctx'), parts along dimension 0
There are 4 independent parts, one for each index of `dp`. A program takes and returns all parts, laid end to end along the dimension named above; an argument that names none is the same for every part. Nothing has to cross between parts.
Inputs may be any that keep to these rules, and one draw needn't show every extreme that they name: `unit_source`: each run of 16 slots (one device's units in the balanced order) holds exactly one unit from every run of 16 units of the packed order; every unit appears once. `doc_lengths`: they sum to 2048; the longest is exactly 1024.
All inputs are finite; a program needn't handle non-finite values.
Results may differ from a plain program's by a relative error of at most 0.017.
Values may be sent and summed in bfloat16 or wider, within the bound.
A program may use at most 64 MiB of HBM per device.

v0:
```python
import jax
import jax.numpy as jnp
from jax import lax
from jax.sharding import PartitionSpec as P

HD = 128


def doc_index(positions, doc_ends):
    return jnp.sum((positions[None, :] >= doc_ends[:, None]).astype(jnp.int32), axis=0)


def local(queries, key_rows, value_rows, doc_lengths, unit_source, w_out):
    ctx_count = lax.axis_size("ctx")
    ctx_index = lax.axis_index("ctx")
    tok_dev, columns = queries.shape
    unit_rows = tok_dev // ctx_count
    head_count = columns // HD
    kv_heads = key_rows.shape[1] // HD
    group_size = head_count // kv_heads
    unit_plan = unit_source.reshape(ctx_count, ctx_count)
    wanted = unit_plan // ctx_count == ctx_index
    send_order = jnp.sum(jnp.where(wanted, unit_plan % ctx_count, 0), axis=1)
    outgoing = jnp.take(queries.reshape(ctx_count, unit_rows, columns), send_order, axis=0)
    incoming = lax.all_to_all(outgoing, "ctx", split_axis=0, concat_axis=0, tiled=True)
    my_units = lax.dynamic_index_in_dim(unit_plan, ctx_index, 0, keepdims=False)
    arranged = jnp.take(incoming, my_units // ctx_count, axis=0).reshape(tok_dev, columns)
    positions = (
        my_units[:, None] * unit_rows + jnp.arange(unit_rows, dtype=jnp.int32)[None, :]
    ).reshape(tok_dev)
    doc_ends = jnp.cumsum(doc_lengths)
    query_doc = doc_index(positions, doc_ends)
    grouped = arranged.reshape(tok_dev, kv_heads, group_size, HD)
    score_scale = HD ** (-0.5)
    state_shape = (kv_heads, group_size, tok_dev)
    run_max = jnp.full(state_shape, -1e30, jnp.float32)
    key_piece = lax.all_gather(key_rows, "ctx", axis=0, tiled=True)
    value_piece = lax.all_gather(value_rows, "ctx", axis=0, tiled=True)
    extent = key_piece.shape[0]
    key_pos = jnp.arange(extent, dtype=jnp.int32)
    key_doc = doc_index(key_pos, doc_ends)
    visible = (key_doc[None, :] == query_doc[:, None]) & (key_pos[None, :] <= positions[:, None])
    scores = (
        jnp.einsum(
            "qkgd,pkd->kgqp",
            grouped,
            key_piece.reshape(extent, kv_heads, HD),
            preferred_element_type=jnp.float32,
        )
        * score_scale
    )
    scores = jnp.where(visible, scores, -1e30)
    new_max = jnp.maximum(run_max, jnp.max(scores, axis=3))
    weights = jnp.where(visible, jnp.exp(scores - new_max[..., None]), 0.0)
    new_sum = jnp.sum(weights, axis=3)
    blended = jnp.einsum(
        "kgqp,pkd->kgqd",
        weights.astype(jnp.bfloat16),
        value_piece.reshape(extent, kv_heads, HD),
        preferred_element_type=jnp.float32,
    )
    attended = (
        (blended / new_sum[..., None])
        .transpose(2, 0, 1, 3)
        .reshape(tok_dev, columns)
        .astype(jnp.bfloat16)
    )
    partial_value = jnp.dot(
        lax.all_gather(attended, "ctx", axis=0, tiled=True),
        w_out,
        preferred_element_type=jnp.float32,
    )
    summed = lax.psum_scatter(
        partial_value.astype(jnp.bfloat16), "tp", scatter_dimension=0, tiled=True
    )
    return summed


def solution(mesh):
    return jax.shard_map(
        local,
        mesh=mesh,
        in_specs=(
            P(("dp", "ctx"), "tp"),
            P(("dp", "ctx"), "tp"),
            P(("dp", "ctx"), "tp"),
            P("dp"),
            P("dp"),
            P("tp", "ctx"),
        ),
        out_specs=P(("dp", "tp"), "ctx"),
        check_vma=False,
    )
```

profile of v0, /device:TPU:6, one launch (start us, length us, event | category | flops | bytes accessed | tf_op | source)
XLA Modules:
  0.0 227.8 jit_solution(13007387504424359133)
XLA Ops:
  6.5 0.0 copy-start
  6.5 0.9 reshape.108
  7.4 0.1 fusion.20
  7.6 1.5 gather_fusion
  9.1 0.8 broadcast_select_fusion
  9.9 9.2 %all-to-all-start = ((bf16[16,8,1024]{2,1,0:T(8,128)(2,1)}), bf16[16,8,1024]{2,1,0:T(8,128)(2,1)S(1)}, u32[]{:S(2)}, u32[]{:S(2)}) async-start(bf16[16,8,1024]{2,1,0:T(8,128)(2,1)} %broadcast_select_fusion), calls=%async_computation | async-start | bytes 524288 | tf_op jit(solution)/shard_map/all_to_all | solution.py:25
  19.1 0.0 all-gather.2.cloned.1.call-start
  19.2 0.1 iota_add_fusion
  19.3 0.1 add.45
  19.4 0.8 reduce-window.8
  20.2 0.1 convert_reduce_fusion
  20.3 0.1 convert_reduce_fusion.1
  20.4 0.9 copy.11
  21.3 0.4 fusion.7
  21.7 23.7 %all_gather.9 = bf16[2048,128]{1,0:T(8,128)(2,1)S(1)} all-gather(bf16[128,128]{1,0:T(8,128)(2,1)} %param.9), channel_id=1, replica_groups=mesh['ctx'=16,'tp'=8,'dp'=4] {'ctx'}, dimensions={0}, use_global_device_ids=true | all-gather | bytes 557056 | tf_op jit(solution)/shard_map/all_gather | solution.py:37
  45.4 24.4 %all_gather.10 = bf16[2048,128]{0,1:T(8,128)(2,1)} all-gather(bf16[128,128]{0,1:T(8,128)(2,1)S(1)} %copy.11), channel_id=1, replica_groups=mesh['ctx'=16,'tp'=8,'dp'=4] {'ctx'}, dimensions={0}, use_global_device_ids=true | all-gather | bytes 557056 | tf_op jit(solution)/shard_map/all_gather | solution.py:38
  69.8 0.0 all-to-all-done
  69.8 0.6 gather_fusion.1
  70.4 0.1 select_bitcast_fusion
  70.5 0.0 copy-start.1
  70.5 1.7 fusion
  72.2 2.5 %fusion.1 = f32[8,128]{1,0:T(8,128)S(1)} fusion(f32[128,8,2048]{2,0,1:T(8,128)S(1)} %get-tuple-element.9, f32[8,128]{1,0:T(8,128)S(1)} %broadcast_maximum_fusion, pred[128,2048]{1,0:T(8,128)(4,1)S(1)} %fusion.7), kind=kLoop, calls=%fused_computation.5 | loop fusion | flops 10484736 | bytes 8658944 | tf_op jit(solution)/shard_map/reduce_sum | solution.py:55
  74.8 0.0 copy-done.1
  74.8 3.0 %fusion.11 = bf16[8,128,128]{1,2,0:T(8,128)(2,1)} fusion(f32[128,8,2048]{2,0,1:T(8,128)S(1)} %get-tuple-element.9, f32[8,128]{1,0:T(8,128)S(1)} %broadcast_maximum_fusion, pred[128,2048]{1,0:T(8,128)(4,1)S(1)} %fusion.7, bf16[2048,128]{0,1:T(8,128)(2,1)S(1)} %copy-done.1, f32[8,128]{1,0:T(8,128)S(1)} %fusion.1), kind=kOutput, calls=%fused_computation.14 | convolution fusion | flops 547618816 | bytes 9445376 | tf_op jit(solution)/shard_map/kgqp,pkd->kgqd/dot_general | solution.py:56
  77.8 0.0 all-gather.2.cloned.1.call-update
  77.8 0.0 reduce-scatter.2.cloned.1.call-start
  77.8 74.4 %all-gather.2.cloned.1.call-done = bf16[2048,1024]{0,1:T(8,128)(2,1)} async-done(((bf16[128,1024]{0,1:T(8,128)(2,1)}), bf16[2048,1024]{0,1:T(8,128)(2,1)}) %all-gather.2.cloned.1.call-update) | async-done | bytes 4194320 | tf_op jit(solution)/shard_map/all_gather | solution.py:69
  152.2 0.0 copy-done
  152.2 8.4 %convolution_convert_fusion = bf16[2048,1024]{1,0:T(8,128)(2,1)} fusion(bf16[2048,1024]{0,1:T(8,128)(2,1)} %all-gather.2.cloned.1.call-done, bf16[1024,1024]{1,0:T(8,128)(2,1)S(1)} %copy-done), kind=kOutput, calls=%fused_computation.10 | convolution fusion | flops 4297064448 | bytes 10485760 | tf_op jit(solution)/shard_map/dot_general | solution.py:68
  160.6 0.0 reduce-scatter.2.cloned.1.call-update
  160.6 60.4 %reduce-scatter.2.cloned.1.call-done = bf16[256,1024]{1,0:T(8,128)(2,1)} async-done(((bf16[2048,1024]{1,0:T(8,128)(2,1)}), bf16[256,1024]{1,0:T(8,128)(2,1)}) %reduce-scatter.2.cloned.1.call-update) | async-done | bytes 524304 | tf_op jit(solution)/shard_map/reduce_scatter | solution.py:73
  (8 shorter events, 0.1 us)
Async XLA Ops:
  6.5 145.7 %copy-start = (bf16[1024,1024]{1,0:T(8,128)(2,1)S(1)}, bf16[1024,1024]{1,0:T(8,128)(2,1)}, u32[]{:S(2)}) copy-start(bf16[1024,1024]{1,0:T(8,128)(2,1)} %param.13) | copy-start | bytes 6291460
  9.9 59.9 %all-to-all-start = ((bf16[16,8,1024]{2,1,0:T(8,128)(2,1)}), bf16[16,8,1024]{2,1,0:T(8,128)(2,1)S(1)}, u32[]{:S(2)}, u32[]{:S(2)}) async-start(bf16[16,8,1024]{2,1,0:T(8,128)(2,1)} %broadcast_select_fusion), calls=%async_computation | async-start | bytes 524288 | tf_op jit(solution)/shard_map/all_to_all | solution.py:25
  19.1 133.1 %all-gather.2.cloned.1.call-start = ((), (), s32[]{:S(2)}) async-start(), calls=%async_computation.2 | async-start | bytes 4456448 | tf_op jit(solution)/shard_map/all_gather | solution.py:69
  70.5 4.2 %copy-start.1 = (bf16[2048,128]{0,1:T(8,128)(2,1)S(1)}, bf16[2048,128]{0,1:T(8,128)(2,1)}, u32[]{:S(2)}) copy-start(bf16[2048,128]{0,1:T(8,128)(2,1)} %all_gather.10) | copy-start | bytes 1572868
  77.8 143.2 %reduce-scatter.2.cloned.1.call-start = ((), (), s32[]{:S(2)}) async-start(), calls=%async_computation.3 | async-start | bytes 4718592 | tf_op jit(solution)/shard_map/reduce_scatter | solution.py:73
Sparse Core Ops, SparseCore 0:
  77.9 74.2 all-gather.1
  160.8 60.1 reduce-scatter.1
where the time goes:
time: 228 us
  waiting for transfers between devices  135 us (59%)
  blocking collectives  48.1 us (21%)
  between operations  13.5 us (6%)
  matrix products  13.1 us (6%)
  starting transfers between devices  9.26 us (4%)
  other arithmetic  5.11 us (2%)
  local copies, waits for them, and re-layouts  3.98 us (2%)
    all_gather x1, waiting for transfers between devices, local(): lax.all_gather(attended, 'ctx', axis=0, tiled=True)  74.4 us
    reduce_scatter x1, waiting for transfers between devices, local(): lax.psum_scatter(partial_value.astype(jnp.bfloat16), 'tp', scatter_dimens...  60.4 us
    all_gather x1, blocking collectives, local(): value_piece = lax.all_gather(value_rows, 'ctx', axis=0, tiled=True)  24.4 us
    all_gather x1, blocking collectives, local(): key_piece = lax.all_gather(key_rows, 'ctx', axis=0, tiled=True)  23.7 us
    all_to_all x1, starting transfers between devices, local(): lax.all_to_all(outgoing, 'ctx', split_axis=0, concat_axis=0, tiled=True)  9.19 us
    dot_general x1, matrix products, local(): jnp.dot(lax.all_gather(attended, 'ctx', axis=0, tiled=True), w_out, prefe...  8.4 us
  transfers between devices with their start and end apart: 3, of which 2 were waited for; matrix products, arithmetic and copies ran while one was open for 1% of the time, Pallas kernels for 0%

commit v1 on v0

v1 whole, which is shorter than its diff:
```python
import functools

import jax
import jax.numpy as jnp
from jax import lax
from jax.experimental import pallas as pl
from jax.experimental.pallas import tpu as pltpu
from jax.sharding import PartitionSpec as P

HD = 128
UNIT = 8
SPAN = 9
MESH = pl.DeviceIdType.MESH


def kernel(
    lengths_ref, units_ref, q_ref, k_ref, v_ref, w_ref, out_ref,
    kv_buf, slots, w_buf, q_in, order, out_order, q_heads, pos_buf, bias, k_cat, v_cat, att,
    part_out, part_in,
    load_sem, w_send, w_recv, kv_send, kv_recv, ag_send, ag_recv,
    give_send, give_recv, rs_send, rs_recv,
):
    ctx, tp, dp = lax.axis_index("ctx"), lax.axis_index("tp"), lax.axis_index("dp")
    y, x = ctx // 4, ctx % 4
    zl, core = tp // 2, tp % 2
    sign = 1 - 2 * core

    def at_plane(yy, xx):
        return {"ctx": ((yy + 4) % 4) * 4 + (xx + 4) % 4}

    def at_z(step):
        moved = zl + step + 4
        return {"tp": (moved % 4) * 2 + core, "dp": (dp + moved // 4 + 3) % 4}

    def at_part(step, c):
        return {"tp": zl * 2 + c, "dp": (dp + step + 4) % 4}

    x_next, x_prev = at_plane(y, x + 1), at_plane(y, x - 1)
    y_next, y_prev = at_plane(y + 1, x), at_plane(y - 1, x)
    twin = {"tp": zl * 2 + 1 - core}

    loads = [
        pltpu.make_async_copy(k_ref, kv_buf.at[0, y, x], load_sem.at[0]),
        pltpu.make_async_copy(v_ref, kv_buf.at[1, x, y], load_sem.at[1]),
        pltpu.make_async_copy(q_ref, q_in, load_sem.at[2]),
        pltpu.make_async_copy(w_ref, w_buf.at[core], load_sem.at[3]),
    ]
    for load in loads:
        load.start()

    barrier = pltpu.get_barrier_semaphore()
    partners = [
        x_next, x_prev, y_next, y_prev, twin, at_z(1), at_z(-1),
        at_part(1, core), at_part(-1, core), at_part(1, 1 - core), at_part(-1, 1 - core),
    ]
    for partner in partners:
        pl.semaphore_signal(barrier, inc=1, device_id=partner, device_id_type=MESH)
    pl.semaphore_wait(barrier, len(partners))

    def gather_copies(buf, send, recv):
        copies = {}
        for half in range(2):
            first, second = (x, y) if half == 0 else (y, x)
            first_to = (x_next, x_prev) if half == 0 else (y_next, y_prev)
            second_to = (y_next, y_prev) if half == 0 else (x_next, x_prev)
            for way in range(2):
                back = 3 if way == 0 else 1
                regions = (
                    (buf.at[half, second, first], first_to[way]),
                    (buf.at[half, second, (first + back) % 4, way], first_to[way]),
                    (buf.at[half, second], second_to[way]),
                    (buf.at[half, (second + back) % 4, :, way], second_to[way]),
                )
                for stage, (region, target) in enumerate(regions):
                    copies[half, stage, way] = pltpu.make_async_remote_copy(
                        src_ref=region,
                        dst_ref=region,
                        send_sem=send.at[half, stage, way],
                        recv_sem=recv.at[half, stage, way],
                        device_id=target,
                        device_id_type=MESH,
                    )
        return copies

    def begin(copies, stage):
        for way in range(2):
            for half in range(2):
                copies[half, stage, way].start()

    def arrive(copies, stage):
        for way in range(2):
            for half in range(2):
                copies[half, stage, way].wait_recv()

    def sent(copies):
        for copy in copies.values():
            copy.wait_send()

    kv = gather_copies(kv_buf, kv_send, kv_recv)
    loads[0].wait()
    loads[1].wait()
    begin(kv, 0)
    w_copy = pltpu.make_async_remote_copy(
        src_ref=w_ref, dst_ref=w_buf.at[core], send_sem=w_send, recv_sem=w_recv,
        device_id=twin, device_id_type=MESH,
    )
    w_copy.start()
    arrive(kv, 0)
    begin(kv, 1)

    row8 = lax.broadcasted_iota(jnp.int32, (UNIT, HD), 0)
    lane8 = lax.broadcasted_iota(jnp.int32, (UNIT, HD), 1)

    def place(d, carry):
        unit = jnp.zeros((UNIT, HD), jnp.int32)
        for i in range(16):
            value = jnp.full((UNIT, HD), units_ref[d * 16 + i])
            unit = jnp.where(lax.shift_right_logical(value, 4) == ctx, value & 15, unit)
        row = unit * UNIT + row8
        rows = pl.ds(pl.multiple_of(d * UNIT, UNIT), UNIT)
        pos_buf[rows, :] = ctx * 128 + row
        order[rows, :] = (lane8 == row).astype(jnp.float32)
        return carry

    lax.fori_loop(0, 16, place, 0)
    for n in range(32):
        value = jnp.full((UNIT, HD), units_ref[tp * 32 + n])
        row = lax.shift_right_logical(value, 4) * 16 + (n // 16) * UNIT + row8
        for side in range(2):
            out_order[n * UNIT:(n + 1) * UNIT, side * HD:(side + 1) * HD] = (
                lane8 + side * HD == row
            ).astype(jnp.float32)
    arrive(kv, 1)
    begin(kv, 2)
    loads[2].wait()
    ordered = jnp.dot(
        order[...].astype(jnp.bfloat16), q_in[...], preferred_element_type=jnp.float32
    ).astype(jnp.bfloat16)
    for head in range(8):
        q_heads[head] = ordered[:, head * HD:(head + 1) * HD]
    pos = pos_buf[...]
    begins = jnp.zeros_like(pos)
    end = jnp.int32(0)
    for j in range(8):
        end = end + lengths_ref[j]
        begins = jnp.where(pos >= end, end, begins)
    lane = lax.broadcasted_iota(jnp.int32, (128, HD), 1)
    for block in range(SPAN):
        key_pos = (ctx - (SPAN - 1) + block) * 128 + lane
        seen = (key_pos >= begins) & (key_pos <= pos)
        bias[:, block * 128:(block + 1) * 128] = jnp.where(seen, 0.0, -1e30)
    v_cat[:, HD:] = jnp.ones((SPAN * 128, HD), jnp.bfloat16)
    arrive(kv, 2)
    begin(kv, 3)
    arrive(kv, 3)
    for block in range(SPAN):
        other = (ctx + 16 - (SPAN - 1) + block) % 16
        oy, ox = other // 4, other % 4
        for part in range(2):
            rows = slice(block * 128 + part * 64, block * 128 + part * 64 + 64)
            k_cat[rows, :] = kv_buf[0, oy, ox, part]
            v_cat[rows, :HD] = kv_buf[1, ox, oy, part]

    factor = (HD ** -0.5) * 1.4426950408889634
    for pair in range(4):
        two = jnp.concatenate([q_heads[2 * pair], q_heads[2 * pair + 1]], axis=0)
        scores = lax.dot_general(
            two, k_cat[...], (((1,), (1,)), ((), ())),
            preferred_element_type=jnp.float32,
        )
        masked = jnp.concatenate([scores[:128] + bias[...], scores[128:] + bias[...]], axis=0)
        top = jnp.max(masked, axis=1, keepdims=True)
        weights = jnp.exp2((masked - top) * factor).astype(jnp.bfloat16)
        blended = jnp.dot(weights, v_cat[...], preferred_element_type=jnp.float32)
        result = (blended[:, :HD] / blended[:, HD:]).astype(jnp.bfloat16)
        for one in range(2):
            head = 2 * pair + one
            col = (head % 4) * HD
            att[:, head // 4, :, col:col + HD] = result[one * 128:(one + 1) * 128].reshape(8, 16, HD)

    def chunk_step(k, s):
        return (-s, 2 * s, s, 0 * s)[k]

    def give(k, c):
        s = 1 - 2 * c
        shifted = zl + chunk_step(k, s) + 4
        block = shifted % 4
        ahead = 1 - shifted // 4
        return att.at[2 * block + c], ahead

    given, kept, gone = {}, {}, {}
    halves = (slots.at[:, 0, y, x], slots.at[:, 1, x, y])

    def slot(k, half_is_core_one):
        return slots.at[k, 1, x, y] if half_is_core_one else slots.at[k, 0, y, x]

    def both(emit):
        for c in range(2):
            pl.when(core == c)(functools.partial(emit, c))

    def start_gifts(k, c):
        rows, ahead = give(k, 1 - c)
        pltpu.make_async_remote_copy(
            src_ref=rows, dst_ref=slot(k, c == 1), send_sem=give_send.at[k, 1],
            recv_sem=give_recv.at[k, c], device_id=at_part(ahead, 1 - c), device_id_type=MESH,
        ).start()
        rows, ahead = give(k, c)

        @pl.when(ahead == 0)
        def _():
            pltpu.make_async_copy(rows, slot(k, c == 1), give_recv.at[k, c]).start()

        @pl.when(ahead != 0)
        def _():
            pltpu.make_async_remote_copy(
                src_ref=rows, dst_ref=slot(k, c == 1), send_sem=give_send.at[k, 0],
                recv_sem=give_recv.at[k, c], device_id=at_part(ahead, c), device_id_type=MESH,
            ).start()

    def end_gifts(k, c):
        rows, ahead = give(k, c)
        pltpu.make_async_copy(rows, rows, give_send.at[k, 1]).wait()

        @pl.when(ahead != 0)
        def _():
            pltpu.make_async_copy(rows, rows, give_send.at[k, 0]).wait()

    def gifts_in(k):
        for half in range(2):
            pltpu.make_async_copy(att.at[0], slot(k, half == 1), give_recv.at[k, half]).wait()

    for k in range(4):
        both(functools.partial(start_gifts, k))

    gathers = [gather_copies(slots.at[k], ag_send.at[k], ag_recv.at[k]) for k in range(4)]

    def s1(k):
        gifts_in(k)
        begin(gathers[k], 0)

    def s2(k):
        arrive(gathers[k], 0)
        begin(gathers[k], 1)

    def s3(k):
        arrive(gathers[k], 1)
        begin(gathers[k], 2)

    def s4(k):
        arrive(gathers[k], 2)
        begin(gathers[k], 3)

    def hand_on(k, j):
        step = (-sign, sign, sign)[k]
        return pltpu.make_async_remote_copy(
            src_ref=part_out.at[k, j], dst_ref=part_in.at[k, j],
            send_sem=rs_send.at[k, j], recv_sem=rs_recv.at[k, j],
            device_id=at_z(step), device_id_type=MESH,
        )

    def project(k):
        arrive(gathers[k], 3)

        def tile(j, carry):
            cols = pl.ds(pl.multiple_of(j * 256, 256), 256)
            acc = jnp.zeros((256, 256), jnp.float32)
            for half in range(2):
                for part in range(2):
                    left = jnp.concatenate(
                        [
                            slots[k, half, a, b, part]
                            for a, b in (
                                (n // 4, n % 4) if half == 0 else (n % 4, n // 4) for n in range(16)
                            )
                        ],
                        axis=0,
                    )
                    acc = acc + jnp.dot(
                        left, w_buf[half, part * 512:(part + 1) * 512, cols],
                        preferred_element_type=jnp.float32,
                    )
            if k == 2:
                hand_on(1, j).wait_recv()
                acc = acc + part_in[1, j].astype(jnp.float32)
            if k == 3:
                hand_on(0, j).wait_recv()
                hand_on(2, j).wait_recv()
                acc = acc + part_in[0, j].astype(jnp.float32) + part_in[2, j].astype(jnp.float32)
                out_ref[:, cols] = jnp.dot(
                    out_order[...].astype(jnp.bfloat16), acc.astype(jnp.bfloat16),
                    preferred_element_type=jnp.float32,
                ).astype(jnp.bfloat16)
            else:
                part_out[k, j] = acc.astype(jnp.bfloat16)
                hand_on(k, j).start()
            return carry

        lax.fori_loop(0, 4, tile, 0)

    s1(0)
    s2(0)
    s1(1)
    s3(0)
    s2(1)
    s1(2)
    s4(0)
    s3(1)
    s2(2)
    s1(3)
    w_copy.wait()
    loads[3].wait()
    project(0)
    s4(1)
    s3(2)
    s2(3)
    project(1)
    s4(2)
    s3(3)
    project(2)
    s4(3)
    sent(kv)
    for k in range(4):
        both(functools.partial(end_gifts, k))
    for k in range(3):
        sent(gathers[k])
    project(3)

    sent(gathers[3])
    for k in range(3):
        for j in range(4):
            hand_on(k, j).wait_send()


def local(queries, key_rows, value_rows, doc_lengths, unit_source, w_out):
    bf16, f32, i32 = jnp.bfloat16, jnp.float32, jnp.int32
    dma = pltpu.SemaphoreType.DMA
    vmem = pltpu.VMEM
    anywhere = pl.BlockSpec(memory_space=pl.ANY)
    smem = pl.BlockSpec(memory_space=pltpu.SMEM)
    return pl.pallas_call(
        kernel,
        out_shape=jax.ShapeDtypeStruct((256, 1024), bf16),
        in_specs=[smem, smem, anywhere, anywhere, anywhere, anywhere],
        out_specs=pl.BlockSpec(memory_space=pltpu.VMEM),
        scratch_shapes=[
            vmem((2, 4, 4, 2, 64, HD), bf16),
            vmem((4, 2, 4, 4, 2, 16, 512), bf16),
            vmem((2, 1024, 1024), bf16),
            vmem((128, 1024), bf16),
            vmem((128, HD), f32),
            vmem((256, 256), f32),
            vmem((8, 128, HD), bf16),
            vmem((128, HD), i32),
            vmem((128, SPAN * 128), f32),
            vmem((SPAN * 128, HD), bf16),
            vmem((SPAN * 128, 2 * HD), bf16),
            vmem((8, 2, 16, 512), bf16),
            vmem((3, 4, 256, 256), bf16),
            vmem((3, 4, 256, 256), bf16),
            dma((4,)),
            dma,
            dma,
            dma((2, 4, 2)),
            dma((2, 4, 2)),
            dma((4, 2, 4, 2)),
            dma((4, 2, 4, 2)),
            dma((4, 2)),
            dma((4, 2)),
            dma((3, 4)),
            dma((3, 4)),
        ],
        compiler_params=pltpu.CompilerParams(
            collective_id=0, has_side_effects=True, vmem_limit_bytes=44 << 20
        ),
        cost_estimate=pl.CostEstimate(
            flops=5_500_000_000, bytes_accessed=8_000_000, transcendentals=1_200_000
        ),
    )(
        doc_lengths, unit_source, queries,
        key_rows.reshape(2, 64, HD), value_rows.reshape(2, 64, HD), w_out,
    )


def solution(mesh):
    return jax.shard_map(
        local,
        mesh=mesh,
        in_specs=(
            P(("dp", "ctx"), "tp"),
            P(("dp", "ctx"), "tp"),
            P(("dp", "ctx"), "tp"),
            P("dp"),
            P("dp"),
            P("tp", "ctx"),
        ),
        out_specs=P(("dp", "tp"), "ctx"),
        check_vma=False,
    )
```

time: 228 us -> 82.3 us (0.36)
  waiting for transfers between devices: 135 us -> 0 us
  Pallas kernels: 0 us -> 74.7 us
  blocking collectives: 48.1 us -> 0 us
  between operations: 13.5 us -> 0.02 us
  matrix products: 13.1 us -> 0 us
  starting transfers between devices: 9.26 us -> 0 us
  other arithmetic: 5.11 us -> 0 us
    pallas_call x0 -> x1, Pallas kernels: none -> 74.7 us  [local(): pl.pallas_call(kernel, out_shape=jax.ShapeDtypeStruct((256, 1024), bf16),...]
    all_gather x1 -> x0, waiting for transfers between devices: 74.4 us -> none  [local(): lax.all_gather(attended, 'ctx', axis=0, tiled=True)]
    reduce_scatter x1 -> x0, waiting for transfers between devices: 60.4 us -> none  [local(): lax.psum_scatter(partial_value.astype(jnp.bfloat16), 'tp', scatter_dimens...]
    all_gather x2 -> x0, blocking collectives: 48.1 us -> none  [the longest x1 24.4 us: local(): value_piece = lax.all_gather(value_rows, 'ctx', axis=0, tiled=True)]
    dot_general x3 -> x0, matrix products: 13.1 us -> none  [the longest x1 8.4 us: local(): jnp.dot(lax.all_gather(attended, 'ctx', axis=0, tiled=True), w_out, prefe...]
    all_to_all x1 -> x0, starting transfers between devices: 9.19 us -> none  [local(): lax.all_to_all(outgoing, 'ctx', split_axis=0, concat_axis=0, tiled=True)]
    unnamed x6 -> x13, local copies, waits for them, and re-layouts: 0.91 us -> 6.18 us
    reduce_sum x4 -> x0, other arithmetic: 2.81 us -> none  [the longest x1 2.51 us: local(): new_sum = jnp.sum(weights, axis=3)]
  transfers between devices with their start and end apart: 3 -> 0, of which waited for: 2 -> 0; matrix products, arithmetic and copies ran while one was open for 1% -> 0% of each run, Pallas kernels for 0% -> 0%
where the time goes in v1:
time: 82.3 us; the launch traced here: 80.9 us
  Pallas kernels  74.7 us (91%)
  local copies, waits for them, and re-layouts  6.18 us (8%)
    pallas_call x1, Pallas kernels, local(): pl.pallas_call(kernel, out_shape=jax.ShapeDtypeStruct((256, 1024), bf16),...  74.7 us
    unnamed x13, local copies, waits for them, and re-layouts  6.18 us

profile of v1, /device:TPU:6, one launch (start us, length us, event | category | flops | bytes accessed | tf_op | source)
XLA Modules:
  0.0 80.9 jit_solution(9156785546488935600)
XLA Ops:
  0.0 0.0 copy-start
  0.0 1.6 %copy-done = bf16[1024,1024]{1,0:T(8,128)(2,1)S(1)} copy-done((bf16[1024,1024]{1,0:T(8,128)(2,1)S(1)}, bf16[1024,1024]{1,0:T(8,128)(2,1)}, u32[]{:S(2)}) %copy-start) | copy-done | bytes 2097176
  1.6 0.0 copy-start.1
  1.6 0.9 %copy-done.1 = bf16[128,1024]{1,0:T(8,128)(2,1)S(1)} copy-done((bf16[128,1024]{1,0:T(8,128)(2,1)S(1)}, bf16[128,1024]{1,0:T(8,128)(2,1)}, u32[]{:S(2)}) %copy-start.1) | copy-done | bytes 262168
  2.5 0.0 copy-start.2
  2.5 0.8 copy-done.2
  3.3 0.0 copy-start.3
  3.3 0.8 copy-done.3
  4.1 0.0 copy-start.4
  4.1 0.7 copy-done.4
  4.7 0.0 copy-start.5
  4.7 0.7 copy-done.5
  5.4 74.7 %shard_map.64 = bf16[256,1024]{1,0:T(8,128)(2,1)S(1)} custom-call(s32[8]{0:T(128)S(1)} %copy-done.5, s32[256]{0:T(256)S(1)} %copy-done.4, bf16[128,1024]{1,0:T(8,128)(2,1)S(1)} %copy-done.1, bf16[2,64,128]{2,1,0:T(8,128)(2,1)S(1)} %bitcast.2, bf16[2,64,128]{2,1,0:T(8,128)(2,1)S(1)} %bitcast.3, bf16[1024,1024]{1,0:T(8,128)(2,1)S(1)} %copy-done), custom_call_target="tpu_custom_call" | custom-call | flops 5500000256 | bytes 8000000 | tf_op jit(solution)/shard_map/pallas_call | solution.py:340
  80.1 0.8 copy.8
Async XLA Ops:
  0.0 1.6 %copy-start = (bf16[1024,1024]{1,0:T(8,128)(2,1)S(1)}, bf16[1024,1024]{1,0:T(8,128)(2,1)}, u32[]{:S(2)}) copy-start(bf16[1024,1024]{1,0:T(8,128)(2,1)} %w_ref.1) | copy-start | bytes 6291460
  1.6 0.9 %copy-start.1 = (bf16[128,1024]{1,0:T(8,128)(2,1)S(1)}, bf16[128,1024]{1,0:T(8,128)(2,1)}, u32[]{:S(2)}) copy-start(bf16[128,1024]{1,0:T(8,128)(2,1)} %q_ref.1) | copy-start | bytes 786436
  2.5 0.8 copy-start.2
  3.3 0.8 copy-start.3
  4.1 0.7 copy-start.4
  4.7 0.7 copy-start.5

commit v2 on v1

v2 whole, which is shorter than its diff:
```python
import functools

import jax
import jax.numpy as jnp
from jax import lax
from jax.experimental import pallas as pl
from jax.experimental.pallas import tpu as pltpu
from jax.sharding import PartitionSpec as P

HD = 128
UNIT = 8
SPAN = 9
VMEM_BYTES = 63 << 20
PLAN = (
    ("attend", 0, 0), ("attend", 1, 0), ("a", 0, 0), ("attend", 3, 0), ("b", 0, 0), ("a", 3, 0),
    ("attend", 2, 0), ("b", 0, 1), ("b", 0, 2), ("f", 0, 0), ("b", 0, 3), ("a", 1, 0), ("b", 1, 0),
    ("b", 3, 1), ("f", 0, 1), ("f", 0, 2), ("f", 0, 3), ("b", 1, 2), ("b", 1, 1), ("b", 1, 3),
    ("a", 2, 0), ("done", 0, 0), ("mm", 0, 0), ("b", 2, 0), ("f", 1, 2), ("mm", 0, 1), ("f", 1, 1),
    ("f", 1, 0), ("mm", 0, 2), ("f", 1, 3), ("b", 2, 1), ("mm", 0, 3), ("b", 2, 2), ("b", 2, 3),
    ("f", 2, 0), ("b", 3, 2), ("b", 3, 0), ("done", 1, 0), ("mm", 1, 0), ("mm", 1, 1), ("f", 2, 1),
    ("mm", 1, 2), ("mm", 1, 3), ("f", 2, 2), ("f", 2, 3), ("f", 3, 2), ("b", 3, 3), ("f", 3, 0),
    ("done", 2, 0), ("mm", 2, 0), ("f", 3, 1), ("mm", 2, 1), ("mm", 2, 2), ("mm", 2, 3),
    ("f", 3, 3), ("done", 3, 0), ("mm", 3, 0), ("mm", 3, 1), ("mm", 3, 2), ("mm", 3, 3),
)
MESH = pl.DeviceIdType.MESH


def kernel(
    lengths_in, units_in, q_ref, k_ref, v_ref, w_ref, out_ref,
    lengths_ref, units_ref, kv_buf, slots, w_buf, q_in, order, out_order, q_rows, pos_buf,
    bias, k_cat, v_cat, att, part_out, part_in, out_tiles,
    load_sem, w_send, w_recv, kv_send, kv_recv, ag_send, ag_recv,
    give_send, give_recv, rs_send, rs_recv, out_sem,
):
    ctx, tp, dp = lax.axis_index("ctx"), lax.axis_index("tp"), lax.axis_index("dp")
    y, x = ctx // 4, ctx % 4
    zl, core = tp // 2, tp % 2
    sign = 1 - 2 * core

    def at_plane(yy, xx):
        return {"ctx": ((yy + 4) % 4) * 4 + (xx + 4) % 4}

    def at_z(step):
        moved = zl + step + 4
        return {"tp": (moved % 4) * 2 + core, "dp": (dp + moved // 4 + 3) % 4}

    def at_part(step, c):
        return {"tp": zl * 2 + c, "dp": (dp + step + 4) % 4}

    x_to = (at_plane(y, x + 1), at_plane(y, x - 1), at_plane(y, x + 2))
    y_to = (at_plane(y + 1, x), at_plane(y - 1, x), at_plane(y + 2, x))
    twin = {"tp": zl * 2 + 1 - core}

    barrier = pltpu.get_barrier_semaphore()
    partners = [
        *x_to, *y_to, twin, at_z(1), at_z(-1),
        at_part(1, core), at_part(-1, core), at_part(1, 1 - core), at_part(-1, 1 - core),
    ]
    for partner in partners:
        pl.semaphore_signal(barrier, inc=1, device_id=partner, device_id_type=MESH)

    loads = [
        pltpu.make_async_copy(k_ref, kv_buf.at[0, y, x], load_sem.at[0]),
        pltpu.make_async_copy(v_ref, kv_buf.at[1, x, y], load_sem.at[1]),
        pltpu.make_async_copy(units_in, units_ref, load_sem.at[2]),
        pltpu.make_async_copy(lengths_in, lengths_ref, load_sem.at[3]),
        pltpu.make_async_copy(q_ref, q_in, load_sem.at[4]),
        pltpu.make_async_copy(w_ref, w_buf.at[core], load_sem.at[5]),
    ]
    for load in loads:
        load.start()

    offsets = (0, 3, 1, 2)

    def gather_copies(buf, send, recv):
        copies = {}
        for half in range(2):
            first, second = (x, y) if half == 0 else (y, x)
            first_to, second_to = (x_to, y_to) if half == 0 else (y_to, x_to)
            regions = []
            for way in range(3):
                regions.append((("a", way), buf.at[half, second, first], first_to[way]))
            for way in range(2):
                line = (second + (3 if way == 0 else 1)) % 4
                for j, offset in enumerate(offsets):
                    place = (first + offset) % 4
                    regions.append((("b", way, j), buf.at[half, second, place], second_to[way]))
                    regions.append((("f", way, j), buf.at[half, line, place, way], second_to[way]))
            for n, (name, region, target) in enumerate(regions):
                copies[(half, *name)] = pltpu.make_async_remote_copy(
                    src_ref=region, dst_ref=region, send_sem=send.at[half, n],
                    recv_sem=recv.at[half, n], device_id=target, device_id_type=MESH,
                )
        return copies

    def e0(g):
        for half in range(2):
            for way in range(2):
                g[half, "a", way].start()
        for half in range(2):
            g[half, "a", 2].start()

    def begin_b(g):
        for half in range(2):
            for way in range(2):
                g[half, "b", way, 0].start()

    def spread(g, way_in, j):
        for half in range(2):
            g[half, "a", way_in].wait_recv()
            for way in range(2):
                g[half, "b", way, j].start()

    def forward(g, j):
        for half in range(2):
            for way in range(2):
                g[half, "b", way, j].wait_recv()
                g[half, "f", way, j].start()

    def e1(g):
        spread(g, 0, 1)
        spread(g, 1, 2)
        forward(g, 0)

    def e2(g):
        spread(g, 2, 3)

    def e3(g):
        forward(g, 1)
        forward(g, 2)

    def e4(g):
        forward(g, 3)

    def e5(g):
        for j in range(4):
            for half in range(2):
                for way in range(2):
                    g[half, "f", way, j].wait_recv()

    def sent(g):
        for copy in g.values():
            copy.wait_send()

    kv = gather_copies(kv_buf, kv_send, kv_recv)
    loads[0].wait()
    loads[1].wait()
    pl.semaphore_wait(barrier, len(partners))

    e0(kv)
    begin_b(kv)
    w_copy = pltpu.make_async_remote_copy(
        src_ref=w_ref, dst_ref=w_buf.at[core], send_sem=w_send, recv_sem=w_recv,
        device_id=twin, device_id_type=MESH,
    )
    w_copy.start()
    loads[2].wait()
    loads[3].wait()

    row8 = lax.broadcasted_iota(jnp.int32, (UNIT, HD), 0)
    lane8 = lax.broadcasted_iota(jnp.int32, (UNIT, HD), 1)

    def place(d, carry):
        unit = jnp.zeros((UNIT, HD), jnp.int32)
        for i in range(16):
            value = jnp.full((UNIT, HD), units_ref[d * 16 + i])
            unit = jnp.where(lax.shift_right_logical(value, 4) == ctx, value & 15, unit)
        row = unit * UNIT + row8
        rows = pl.ds(pl.multiple_of(d * UNIT, UNIT), UNIT)
        pos_buf[rows, :] = ctx * 128 + row
        order[rows, :] = (lane8 == row).astype(jnp.float32)
        return carry

    lax.fori_loop(0, 16, place, 0)
    e1(kv)
    e2(kv)
    loads[4].wait()
    ordered = jnp.dot(
        order[...].astype(jnp.bfloat16), q_in[...], preferred_element_type=jnp.float32
    ).astype(jnp.bfloat16)
    for t in range(8):
        for head in range(8):
            q_rows[t, head * 16:(head + 1) * 16, :] = ordered[
                t * 16:(t + 1) * 16, head * HD:(head + 1) * HD
            ]
    pos = pos_buf[...]
    begins = jnp.zeros_like(pos)
    end = jnp.int32(0)
    for j in range(8):
        end = end + lengths_ref[j]
        begins = jnp.where(pos >= end, end, begins)
    lane = lax.broadcasted_iota(jnp.int32, (128, HD), 1)
    for block in range(SPAN):
        key_pos = (ctx - (SPAN - 1) + block) * 128 + lane
        seen = (key_pos >= begins) & (key_pos <= pos)
        bias[:, :, block * 128:(block + 1) * 128] = jnp.where(seen, 0.0, -1e30).reshape(8, 16, HD)
    v_cat[:, HD:] = jnp.ones((SPAN * 128, HD), jnp.bfloat16)
    e3(kv)
    e4(kv)
    for n in range(32):
        value = jnp.full((UNIT, HD), units_ref[tp * 32 + n])
        row = lax.shift_right_logical(value, 4) * 16 + (n // 16) * UNIT + row8
        for side in range(2):
            out_order[n * UNIT:(n + 1) * UNIT, side * HD:(side + 1) * HD] = (
                lane8 + side * HD == row
            ).astype(jnp.float32)
    e5(kv)
    for block in range(SPAN):
        other = (ctx + 16 - (SPAN - 1) + block) % 16
        oy, ox = other // 4, other % 4
        for part in range(2):
            rows = slice(block * 128 + part * 64, block * 128 + part * 64 + 64)
            k_cat[rows, :] = kv_buf[0, oy, ox, part]
            v_cat[rows, :HD] = kv_buf[1, ox, oy, part]

    def swapped(c):
        return zl == 3 * c

    def rows_for(i, c):
        s = 1 - 2 * c
        if i < 2:
            step = jnp.where(swapped(c), (2 * s, -s)[i], (-s, 2 * s)[i])
        else:
            step = (s, 0)[i - 2]
        shifted = zl + step + 4
        return 2 * (shifted % 4) + c, 1 - shifted // 4

    factor = (HD ** -0.5) * 1.4426950408889634

    def attend(k):
        targets = [rows_for(k, c)[0] for c in (core, 1 - core)]
        two = jnp.concatenate([q_rows[t] for t in targets], axis=0)
        scores = lax.dot_general(
            two, k_cat[...], (((1,), (1,)), ((), ())), preferred_element_type=jnp.float32
        ).reshape(2, 8, 16, SPAN * 128)
        masked = jnp.concatenate(
            [scores[n:n + 1] + bias[t][None, None] for n, t in enumerate(targets)], axis=0
        ).reshape(256, SPAN * 128)
        top = jnp.max(masked, axis=1, keepdims=True)
        weights = jnp.exp2((masked - top) * factor).astype(jnp.bfloat16)
        blended = jnp.dot(weights, v_cat[...], preferred_element_type=jnp.float32)
        result = (blended[:, :HD] / blended[:, HD:]).astype(jnp.bfloat16)
        for n, t in enumerate(targets):
            for head in range(8):
                col = (head % 4) * HD
                at = n * 128 + head * 16
                att[t, head // 4, :, col:col + HD] = result[at:at + 16]

    slot_a = jnp.where(core == 0, y, x)
    slot_b = jnp.where(core == 0, x, y)

    def give_twin(k):
        t, ahead = rows_for(k, 1 - core)
        return pltpu.make_async_remote_copy(
            src_ref=att.at[t], dst_ref=slots.at[k, core, slot_a, slot_b],
            send_sem=give_send.at[k, 1], recv_sem=give_recv.at[k, core],
            device_id=at_part(ahead, 1 - core), device_id_type=MESH,
        )

    def give_part(k):
        t, ahead = rows_for(k, core)
        return ahead, pltpu.make_async_remote_copy(
            src_ref=att.at[t], dst_ref=slots.at[k, core, slot_a, slot_b],
            send_sem=give_send.at[k, 0], recv_sem=give_recv.at[k, core],
            device_id=at_part(ahead, core), device_id_type=MESH,
        )

    def give(k):
        give_twin(k).start()
        ahead, away = give_part(k)
        pl.when(ahead != 0)(away.start)

        @pl.when(ahead == 0)
        def _():
            t, _ = rows_for(k, core)
            pltpu.make_async_copy(
                att.at[t], slots.at[k, core, slot_a, slot_b], give_recv.at[k, core]
            ).start()

    def given(k):
        give_twin(k).wait_send()
        ahead, away = give_part(k)
        pl.when(ahead != 0)(away.wait_send)

    gathers = [gather_copies(slots.at[k], ag_send.at[k], ag_recv.at[k]) for k in range(4)]

    def start(k):
        for half in range(2):
            pltpu.make_async_copy(
                att.at[0], slots.at[k, half, 0, 0], give_recv.at[k, half]
            ).wait()
        e0(gathers[k])

    def hand_on(k, j):
        return pltpu.make_async_remote_copy(
            src_ref=part_out.at[k, j], dst_ref=part_in.at[k, j],
            send_sem=rs_send.at[k, j], recv_sem=rs_recv.at[k, j],
            device_id=at_z(jnp.where(k == 0, -sign, sign)), device_id_type=MESH,
        )

    def store(j):
        cols = pl.ds(pl.multiple_of(j * 256, 256), 256)
        return pltpu.make_async_copy(out_tiles.at[j], out_ref.at[:, cols], out_sem.at[j])

    def project(i, j):
        cols = slice(j * 256, (j + 1) * 256)
        acc = jnp.zeros((256, 256), jnp.float32)
        for half in range(2):
            for part in range(2):
                left = jnp.concatenate(
                    [
                        slots[i, half, a, b, part]
                        for a, b in (
                            (n // 4, n % 4) if half == 0 else (n % 4, n // 4) for n in range(16)
                        )
                    ],
                    axis=0,
                )
                acc = acc + jnp.dot(
                    left, w_buf[half, part * 512:(part + 1) * 512, cols],
                    preferred_element_type=jnp.float32,
                )
        if i == 2:
            hand_on(1, j).wait_recv()
            acc = acc + part_in[1, j].astype(jnp.float32)
        if i == 3:
            hand_on(0, j).wait_recv()
            hand_on(2, j).wait_recv()
            acc = acc + part_in[0, j].astype(jnp.float32) + part_in[2, j].astype(jnp.float32)
            out_tiles[j] = jnp.dot(
                out_order[...].astype(jnp.bfloat16), acc.astype(jnp.bfloat16),
                preferred_element_type=jnp.float32,
            ).astype(jnp.bfloat16)
            store(j).start()
        else:
            k = 2 if i == 2 else jnp.where(swapped(core), 1 - i, i)
            part_out[k, j] = acc.astype(jnp.bfloat16)
            hand_on(k, j).start()

    def step(op, i, j):
        g = gathers[i]
        if op == "attend":
            attend(i)
            give(i)
        elif op == "a":
            start(i)
        elif op == "b":
            if j == 0:
                begin_b(g)
            else:
                spread(g, j - 1, j)
        elif op == "f":
            forward(g, j)
        elif op == "done":
            e5(g)
        else:
            project(i, j)

    for op, i, j in PLAN:
        if op == "mm" and i == 0 and j == 0:
            w_copy.wait()
            loads[5].wait()
        if op == "done" and i == 3:
            sent(kv)
            for n in range(4):
                given(n)
            for n in range(2):
                sent(gathers[n])
        step(op, i, j)
    sent(gathers[2])
    sent(gathers[3])
    for k in range(3):
        for j in range(4):
            hand_on(k, j).wait_send()
    for j in range(4):
        store(j).wait()


def local(queries, key_rows, value_rows, doc_lengths, unit_source, w_out):
    bf16, f32, i32 = jnp.bfloat16, jnp.float32, jnp.int32
    dma = pltpu.SemaphoreType.DMA
    vmem = pltpu.VMEM
    anywhere = pl.BlockSpec(memory_space=pl.ANY)
    return pl.pallas_call(
        kernel,
        out_shape=jax.ShapeDtypeStruct((256, 1024), bf16),
        in_specs=[anywhere] * 6,
        out_specs=anywhere,
        scratch_shapes=[
            pltpu.SMEM((8,), i32),
            pltpu.SMEM((256,), i32),
            vmem((2, 4, 4, 2, 64, HD), bf16),
            vmem((4, 2, 4, 4, 2, 16, 512), bf16),
            vmem((2, 1024, 1024), bf16),
            vmem((128, 1024), bf16),
            vmem((128, HD), f32),
            vmem((256, 256), f32),
            vmem((8, 128, HD), bf16),
            vmem((128, HD), i32),
            vmem((8, 16, SPAN * 128), f32),
            vmem((SPAN * 128, HD), bf16),
            vmem((SPAN * 128, 2 * HD), bf16),
            vmem((8, 2, 16, 512), bf16),
            vmem((3, 4, 256, 256), bf16),
            vmem((3, 4, 256, 256), bf16),
            vmem((4, 256, 256), bf16),
            dma((6,)),
            dma,
            dma,
            dma((2, 19)),
            dma((2, 19)),
            dma((4, 2, 19)),
            dma((4, 2, 19)),
            dma((4, 2)),
            dma((4, 2)),
            dma((3, 4)),
            dma((3, 4)),
            dma((4,)),
        ],
        compiler_params=pltpu.CompilerParams(
            collective_id=0, has_side_effects=True, vmem_limit_bytes=VMEM_BYTES
        ),
        cost_estimate=pl.CostEstimate(
            flops=5_500_000_000, bytes_accessed=8_000_000, transcendentals=1_200_000
        ),
    )(
        doc_lengths, unit_source, queries,
        key_rows.reshape(2, 64, HD), value_rows.reshape(2, 64, HD), w_out,
    )


def solution(mesh):
    return jax.shard_map(
        local,
        mesh=mesh,
        in_specs=(
            P(("dp", "ctx"), "tp"),
            P(("dp", "ctx"), "tp"),
            P(("dp", "ctx"), "tp"),
            P("dp"),
            P("dp"),
            P("tp", "ctx"),
        ),
        out_specs=P(("dp", "tp"), "ctx"),
        check_vma=False,
    )
```

time: 82.3 us -> 72.8 us (0.88); the launches traced: 80.9 us -> 72.6 us
  local copies, waits for them, and re-layouts: 6.18 us -> 1.87 us
  Pallas kernels: 74.7 us -> 70.8 us
    unnamed x13 -> x1, local copies, waits for them, and re-layouts: 6.18 us -> 1.87 us
    pallas_call x1, Pallas kernels: 74.7 us -> 70.8 us  [local(): pl.pallas_call(kernel, out_shape=jax.ShapeDtypeStruct((256, 1024), bf16),...]
where the time goes in v2:
time: 72.8 us; the launch traced here: 72.6 us
  Pallas kernels  70.8 us (97%)
  local copies, waits for them, and re-layouts  1.87 us (3%)
    pallas_call x1, Pallas kernels, local(): pl.pallas_call(kernel, out_shape=jax.ShapeDtypeStruct((256, 1024), bf16),...  70.8 us
    unnamed x1, local copies, waits for them, and re-layouts  1.87 us

profile of v2, /device:TPU:6, one launch (start us, length us, event | category | flops | bytes accessed | tf_op | source)
XLA Modules:
  0.0 72.6 jit_solution(253170217460656113)
XLA Ops:
  0.0 70.8 %shard_map.64 = bf16[256,1024]{1,0:T(8,128)(2,1)} custom-call(s32[8]{0:T(128)} %lengths_in.1, s32[256]{0:T(256)} %units_in.1, bf16[128,1024]{1,0:T(8,128)(2,1)} %q_ref.1, bf16[2,64,128]{2,1,0:T(8,128)(2,1)} %bitcast.2, bf16[2,64,128]{2,1,0:T(8,128)(2,1)} %bitcast.3, bf16[1024,1024]{1,0:T(8,128)(2,1)} %w_ref.1), custom_call_target="tpu_custom_call" | custom-call | flops 5500000256 | bytes 8000000 | tf_op jit(solution)/shard_map/pallas_call | solution.py:384
  70.8 1.9 %copy.8 = bf16[256,1024]{1,0:T(8,128)(2,1)} copy(bf16[256,1024]{1,0:T(8,128)(2,1)} %shard_map.64) | data formatting | bytes 1048576

commit v3 on v2

--- a/solution.py
+++ b/solution.py
@@ -11,16 +11,19 @@
 UNIT = 8
 SPAN = 9
 VMEM_BYTES = 63 << 20
+SOURCES = (0, 1, 2, 3, 4, 5, 7, 8, 12, 13, 15, 6, 9, 10, 11, 14)
+NEAR = 11
 PLAN = (
     ("attend", 0, 0), ("attend", 1, 0), ("a", 0, 0), ("attend", 3, 0), ("b", 0, 0), ("a", 3, 0),
-    ("attend", 2, 0), ("b", 0, 1), ("b", 0, 2), ("f", 0, 0), ("b", 0, 3), ("a", 1, 0), ("b", 1, 0),
-    ("b", 3, 1), ("f", 0, 1), ("f", 0, 2), ("f", 0, 3), ("b", 1, 2), ("b", 1, 1), ("b", 1, 3),
-    ("a", 2, 0), ("done", 0, 0), ("mm", 0, 0), ("b", 2, 0), ("f", 1, 2), ("mm", 0, 1), ("f", 1, 1),
-    ("f", 1, 0), ("mm", 0, 2), ("f", 1, 3), ("b", 2, 1), ("mm", 0, 3), ("b", 2, 2), ("b", 2, 3),
-    ("f", 2, 0), ("b", 3, 2), ("b", 3, 0), ("done", 1, 0), ("mm", 1, 0), ("mm", 1, 1), ("f", 2, 1),
-    ("mm", 1, 2), ("mm", 1, 3), ("f", 2, 2), ("f", 2, 3), ("f", 3, 2), ("b", 3, 3), ("f", 3, 0),
-    ("done", 2, 0), ("mm", 2, 0), ("f", 3, 1), ("mm", 2, 1), ("mm", 2, 2), ("mm", 2, 3),
-    ("f", 3, 3), ("done", 3, 0), ("mm", 3, 0), ("mm", 3, 1), ("mm", 3, 2), ("mm", 3, 3),
+    ("b", 0, 2), ("attend", 2, 0), ("b", 0, 1), ("f", 0, 0), ("b", 0, 3), ("a", 1, 0), ("b", 1, 0),
+    ("f", 0, 1), ("f", 0, 2), ("near", 0, 0), ("f", 0, 3), ("b", 1, 1), ("b", 1, 2), ("f", 1, 0),
+    ("b", 1, 3), ("a", 2, 0), ("done", 0, 0), ("b", 2, 0), ("mm", 0, 0), ("f", 1, 1), ("f", 1, 2),
+    ("mm", 0, 1), ("near", 1, 0), ("f", 1, 3), ("b", 2, 1), ("mm", 0, 2), ("b", 2, 2), ("f", 2, 0),
+    ("b", 2, 3), ("b", 3, 3), ("done", 1, 0), ("b", 3, 0), ("mm", 1, 0), ("b", 3, 2), ("mm", 1, 1),
+    ("b", 3, 1), ("mm", 1, 2), ("mm", 1, 3), ("f", 2, 1), ("f", 2, 2), ("mm", 0, 3), ("f", 2, 3),
+    ("near", 2, 0), ("f", 3, 0), ("done", 2, 0), ("f", 3, 1), ("mm", 2, 0), ("mm", 2, 1),
+    ("mm", 2, 2), ("f", 3, 3), ("mm", 2, 3), ("f", 3, 2), ("done", 3, 0), ("mm", 3, 0),
+    ("mm", 3, 1), ("mm", 3, 2), ("mm", 3, 3),
 )
 MESH = pl.DeviceIdType.MESH
 
@@ -72,7 +75,7 @@
 
     offsets = (0, 3, 1, 2)
 
-    def gather_copies(buf, send, recv):
+    def gather_copies(buf, send, recv, direct=()):
         copies = {}
         for half in range(2):
             first, second = (x, y) if half == 0 else (y, x)
@@ -85,7 +88,11 @@
                 for j, offset in enumerate(offsets):
                     place = (first + offset) % 4
                     regions.append((("b", way, j), buf.at[half, second, place], second_to[way]))
-                    regions.append((("f", way, j), buf.at[half, line, place, way], second_to[way]))
+                    if j in direct:
+                        if way == 0:
+                            regions.append((("d", j), buf.at[half, second, place], second_to[2]))
+                    else:
+                        regions.append((("f", way, j), buf.at[half, line, place, way], second_to[way]))
             for n, (name, region, target) in enumerate(regions):
                 copies[(half, *name)] = pltpu.make_async_remote_copy(
                     src_ref=region, dst_ref=region, send_sem=send.at[half, n],
@@ -100,6 +107,11 @@
         for half in range(2):
             g[half, "a", 2].start()
 
+    def begin_d(g, j):
+        for half in range(2):
+            if (half, "d", j) in g:
+                g[half, "d", j].start()
+
     def begin_b(g):
         for half in range(2):
             for way in range(2):
@@ -110,12 +122,14 @@
             g[half, "a", way_in].wait_recv()
             for way in range(2):
                 g[half, "b", way, j].start()
+        begin_d(g, j)
 
     def forward(g, j):
         for half in range(2):
             for way in range(2):
                 g[half, "b", way, j].wait_recv()
-                g[half, "f", way, j].start()
+                if (half, "f", way, j) in g:
+                    g[half, "f", way, j].start()
 
     def e1(g):
         spread(g, 0, 1)
@@ -132,17 +146,16 @@
     def e4(g):
         forward(g, 3)
 
-    def e5(g):
-        for j in range(4):
-            for half in range(2):
-                for way in range(2):
-                    g[half, "f", way, j].wait_recv()
+    def e5(g, wanted=range(4)):
+        for name, copy in g.items():
+            if (name[1] == "f" and name[3] in wanted) or (name[1] == "d" and name[2] in wanted):
+                copy.wait_recv()
 
     def sent(g):
         for copy in g.values():
             copy.wait_send()
 
-    kv = gather_copies(kv_buf, kv_send, kv_recv)
+    kv = gather_copies(kv_buf, kv_send, kv_recv, (3,))
     loads[0].wait()
     loads[1].wait()
     pl.semaphore_wait(barrier, len(partners))
@@ -197,13 +210,22 @@
     v_cat[:, HD:] = jnp.ones((SPAN * 128, HD), jnp.bfloat16)
     e3(kv)
     e4(kv)
-    for n in range(32):
-        value = jnp.full((UNIT, HD), units_ref[tp * 32 + n])
-        row = lax.shift_right_logical(value, 4) * 16 + (n // 16) * UNIT + row8
+
+    def place_out(n, carry):
+        source = lax.shift_right_logical(jnp.full((UNIT, HD), units_ref[tp * 32 + n]), 4)
+        relative = ((lax.shift_right_logical(source, 2) - y) & 3) * 4 + ((source - x) & 3)
+        rank = jnp.zeros((UNIT, HD), jnp.int32)
+        for r in range(1, 16):
+            rank = jnp.where(relative == SOURCES[r], r, rank)
+        row = rank * 16 + (n // 16) * UNIT + row8
+        rows = pl.ds(pl.multiple_of(n * UNIT, UNIT), UNIT)
         for side in range(2):
-            out_order[n * UNIT:(n + 1) * UNIT, side * HD:(side + 1) * HD] = (
+            out_order[rows, side * HD:(side + 1) * HD] = (
                 lane8 + side * HD == row
             ).astype(jnp.float32)
+        return carry
+
+    lax.fori_loop(0, 32, place_out, 0)
     e5(kv)
     for block in range(SPAN):
         other = (ctx + 16 - (SPAN - 1) + block) % 16
@@ -291,10 +313,13 @@
             ).wait()
         e0(gathers[k])
 
-    def hand_on(k, j):
+    groups = (slice(0, NEAR * 16), slice(NEAR * 16, 256))
+
+    def hand_on(k, j, group):
+        rows = groups[group]
         return pltpu.make_async_remote_copy(
-            src_ref=part_out.at[k, j], dst_ref=part_in.at[k, j],
-            send_sem=rs_send.at[k, j], recv_sem=rs_recv.at[k, j],
+            src_ref=part_out.at[k, j, rows], dst_ref=part_in.at[k, j, rows],
+            send_sem=rs_send.at[k, j, group], recv_sem=rs_recv.at[k, j, group],
             device_id=at_z(jnp.where(k == 0, -sign, sign)), device_id_type=MESH,
         )
 
@@ -302,40 +327,45 @@
         cols = pl.ds(pl.multiple_of(j * 256, 256), 256)
         return pltpu.make_async_copy(out_tiles.at[j], out_ref.at[:, cols], out_sem.at[j])
 
-    def project(i, j):
-        cols = slice(j * 256, (j + 1) * 256)
-        acc = jnp.zeros((256, 256), jnp.float32)
+    at_y = [(y + d) % 4 for d in range(4)]
+    at_x = [(x + d) % 4 for d in range(4)]
+
+    def product(i, j, sources):
+        acc = jnp.zeros((len(sources) * 16, 256), jnp.float32)
         for half in range(2):
             for part in range(2):
-                left = jnp.concatenate(
-                    [
-                        slots[i, half, a, b, part]
-                        for a, b in (
-                            (n // 4, n % 4) if half == 0 else (n % 4, n // 4) for n in range(16)
-                        )
-                    ],
-                    axis=0,
-                )
+                left = []
+                for n in sources:
+                    sy, sx = at_y[n // 4], at_x[n % 4]
+                    left.append(slots[i, half, *((sy, sx) if half == 0 else (sx, sy)), part])
                 acc = acc + jnp.dot(
-                    left, w_buf[half, part * 512:(part + 1) * 512, cols],
+                    jnp.concatenate(left, axis=0),
+                    w_buf[half, part * 512:(part + 1) * 512, j * 256:(j + 1) * 256],
                     preferred_element_type=jnp.float32,
                 )
+        return acc
+
+    def pass_on(i, j, group):
+        rows = groups[group]
+        acc = product(i, j, SOURCES[:NEAR] if group == 0 else SOURCES[NEAR:])
         if i == 2:
-            hand_on(1, j).wait_recv()
-            acc = acc + part_in[1, j].astype(jnp.float32)
-        if i == 3:
-            hand_on(0, j).wait_recv()
-            hand_on(2, j).wait_recv()
-            acc = acc + part_in[0, j].astype(jnp.float32) + part_in[2, j].astype(jnp.float32)
-            out_tiles[j] = jnp.dot(
-                out_order[...].astype(jnp.bfloat16), acc.astype(jnp.bfloat16),
-                preferred_element_type=jnp.float32,
-            ).astype(jnp.bfloat16)
-            store(j).start()
-        else:
-            k = 2 if i == 2 else jnp.where(swapped(core), 1 - i, i)
-            part_out[k, j] = acc.astype(jnp.bfloat16)
-            hand_on(k, j).start()
+            hand_on(1, j, group).wait_recv()
+            acc = acc + part_in[1, j, rows].astype(jnp.float32)
+        k = 2 if i == 2 else jnp.where(swapped(core), 1 - i, i)
+        part_out[k, j, rows] = acc.astype(jnp.bfloat16)
+        hand_on(k, j, group).start()
+
+    def finish(j):
+        acc = product(3, j, SOURCES)
+        for group in range(2):
+            hand_on(0, j, group).wait_recv()
+            hand_on(2, j, group).wait_recv()
+        acc = acc + part_in[0, j].astype(jnp.float32) + part_in[2, j].astype(jnp.float32)
+        out_tiles[j] = jnp.dot(
+            out_order[...].astype(jnp.bfloat16), acc.astype(jnp.bfloat16),
+            preferred_element_type=jnp.float32,
+        ).astype(jnp.bfloat16)
+        store(j).start()
 
     def step(op, i, j):
         g = gathers[i]
@@ -351,13 +381,19 @@
                 spread(g, j - 1, j)
         elif op == "f":
             forward(g, j)
+        elif op == "near":
+            e5(g, (0,))
+            for n in range(4):
+                pass_on(i, n, 0)
         elif op == "done":
-            e5(g)
+            e5(g, range(4) if i == 3 else (1, 2, 3))
+        elif i < 3:
+            pass_on(i, j, 1)
         else:
-            project(i, j)
+            finish(j)
 
     for op, i, j in PLAN:
-        if op == "mm" and i == 0 and j == 0:
+        if op == "near" and i == 0:
             w_copy.wait()
             loads[5].wait()
         if op == "done" and i == 3:
@@ -371,7 +407,8 @@
     sent(gathers[3])
     for k in range(3):
         for j in range(4):
-            hand_on(k, j).wait_send()
+            hand_on(k, j, 0).wait_send()
+            hand_on(k, j, 1).wait_send()
     for j in range(4):
         store(j).wait()
 
@@ -413,8 +450,8 @@
             dma((4, 2, 19)),
             dma((4, 2)),
             dma((4, 2)),
-            dma((3, 4)),
-            dma((3, 4)),
+            dma((3, 4, 2)),
+            dma((3, 4, 2)),
             dma((4,)),
         ],
         compiler_params=pltpu.CompilerParams(

time: 72.8 us -> 70.4 us (0.967)
  Pallas kernels: 70.8 us -> 68.3 us
    pallas_call x1, Pallas kernels: 70.8 us -> 68.3 us  [local(): pl.pallas_call(kernel, out_shape=jax.ShapeDtypeStruct((256, 1024), bf16),...]
where the time goes in v3:
time: 70.4 us; the launch traced here: 70.2 us
  Pallas kernels  68.3 us (97%)
  local copies, waits for them, and re-layouts  1.87 us (3%)
    pallas_call x1, Pallas kernels, local(): pl.pallas_call(kernel, out_shape=jax.ShapeDtypeStruct((256, 1024), bf16),...  68.3 us
    unnamed x1, local copies, waits for them, and re-layouts  1.87 us

profile of v3, /device:TPU:6, one launch (start us, length us, event | category | flops | bytes accessed | tf_op | source)
XLA Modules:
  0.0 70.2 jit_solution(13796412603931051159)
XLA Ops:
  0.0 68.3 %shard_map.64 = bf16[256,1024]{1,0:T(8,128)(2,1)} custom-call(s32[8]{0:T(128)} %lengths_in.1, s32[256]{0:T(256)} %units_in.1, bf16[128,1024]{1,0:T(8,128)(2,1)} %q_ref.1, bf16[2,64,128]{2,1,0:T(8,128)(2,1)} %bitcast.2, bf16[2,64,128]{2,1,0:T(8,128)(2,1)} %bitcast.3, bf16[1024,1024]{1,0:T(8,128)(2,1)} %w_ref.1), custom_call_target="tpu_custom_call" | custom-call | flops 5500000256 | bytes 8000000 | tf_op jit(solution)/shard_map/pallas_call | solution.py:421
  68.3 1.9 %copy.8 = bf16[256,1024]{1,0:T(8,128)(2,1)} copy(bf16[256,1024]{1,0:T(8,128)(2,1)} %shard_map.64) | data formatting | bytes 1048576

commit v4 on v3

--- a/solution.py
+++ b/solution.py
@@ -31,9 +31,9 @@
 def kernel(
     lengths_in, units_in, q_ref, k_ref, v_ref, w_ref, out_ref,
     lengths_ref, units_ref, kv_buf, slots, w_buf, q_in, order, out_order, q_rows, pos_buf,
-    bias, k_cat, v_cat, att, part_out, part_in, out_tiles,
+    bias, k_cat, v_cat, att, part_out, part_in, out_tiles, stage,
     load_sem, w_send, w_recv, kv_send, kv_recv, ag_send, ag_recv,
-    give_send, give_recv, rs_send, rs_recv, out_sem,
+    give_send, give_recv, stage_send, stage_recv, rs_send, rs_recv, out_sem,
 ):
     ctx, tp, dp = lax.axis_index("ctx"), lax.axis_index("tp"), lax.axis_index("dp")
     y, x = ctx // 4, ctx % 4
@@ -56,8 +56,8 @@
 
     barrier = pltpu.get_barrier_semaphore()
     partners = [
-        *x_to, *y_to, twin, at_z(1), at_z(-1),
-        at_part(1, core), at_part(-1, core), at_part(1, 1 - core), at_part(-1, 1 - core),
+        at_part(1, core), at_part(-1, core), at_z(1), at_z(-1), x_to[2], y_to[2],
+        *x_to[:2], *y_to[:2], twin,
     ]
     for partner in partners:
         pl.semaphore_signal(barrier, inc=1, device_id=partner, device_id_type=MESH)
@@ -271,38 +271,65 @@
     slot_a = jnp.where(core == 0, y, x)
     slot_b = jnp.where(core == 0, x, y)
 
-    def give_twin(k):
-        t, ahead = rows_for(k, 1 - core)
+    slot = (core, slot_a, slot_b)
+    other_slot = (1 - core, jnp.where(core == 0, x, y), jnp.where(core == 0, y, x))
+
+    def give_twin(i, relayed):
+        t, _ = rows_for(i, 1 - core)
         return pltpu.make_async_remote_copy(
-            src_ref=att.at[t], dst_ref=slots.at[k, core, slot_a, slot_b],
-            send_sem=give_send.at[k, 1], recv_sem=give_recv.at[k, core],
-            device_id=at_part(ahead, 1 - core), device_id_type=MESH,
+            src_ref=att.at[t], dst_ref=stage.at[i] if relayed else slots.at[i, *slot],
+            send_sem=give_send.at[i, 1],
+            recv_sem=stage_recv.at[i] if relayed else give_recv.at[i, core],
+            device_id=twin, device_id_type=MESH,
         )
 
-    def give_part(k):
-        t, ahead = rows_for(k, core)
-        return ahead, pltpu.make_async_remote_copy(
-            src_ref=att.at[t], dst_ref=slots.at[k, core, slot_a, slot_b],
-            send_sem=give_send.at[k, 0], recv_sem=give_recv.at[k, core],
+    def give_part(i):
+        t, ahead = rows_for(i, core)
+        return pltpu.make_async_remote_copy(
+            src_ref=att.at[t], dst_ref=slots.at[i, *slot],
+            send_sem=give_send.at[i, 0], recv_sem=give_recv.at[i, core],
             device_id=at_part(ahead, core), device_id_type=MESH,
         )
 
-    def give(k):
-        give_twin(k).start()
-        ahead, away = give_part(k)
-        pl.when(ahead != 0)(away.start)
+    def relay(i):
+        _, ahead = rows_for(i, core)
+        return pltpu.make_async_remote_copy(
+            src_ref=stage.at[i], dst_ref=slots.at[i, *other_slot],
+            send_sem=stage_send.at[i], recv_sem=give_recv.at[i, 1 - core],
+            device_id=at_part(ahead, core), device_id_type=MESH,
+        )
+
+    def give(i):
+        if i in (0, 3):
+            give_twin(i, False).start()
+        else:
+            _, twin_ahead = rows_for(i, 1 - core)
+            pl.when(twin_ahead == 0)(give_twin(i, False).start)
+            pl.when(twin_ahead != 0)(give_twin(i, True).start)
+        t, ahead = rows_for(i, core)
+        if i in (1, 2):
+            pl.when(ahead != 0)(give_part(i).start)
 
         @pl.when(ahead == 0)
         def _():
-            t, _ = rows_for(k, core)
             pltpu.make_async_copy(
-                att.at[t], slots.at[k, core, slot_a, slot_b], give_recv.at[k, core]
+                att.at[t], slots.at[i, *slot], give_recv.at[i, core]
             ).start()
 
-    def given(k):
-        give_twin(k).wait_send()
-        ahead, away = give_part(k)
-        pl.when(ahead != 0)(away.wait_send)
+    def pass_rows(i):
+        _, ahead = rows_for(i, core)
+
+        @pl.when(ahead != 0)
+        def _():
+            pltpu.make_async_copy(att.at[0], stage.at[i], stage_recv.at[i]).wait()
+            relay(i).start()
+
+    def given(i):
+        give_twin(i, False).wait_send()
+        if i in (1, 2):
+            _, ahead = rows_for(i, core)
+            pl.when(ahead != 0)(give_part(i).wait_send)
+            pl.when(ahead != 0)(relay(i).wait_send)
 
     gathers = [gather_copies(slots.at[k], ag_send.at[k], ag_recv.at[k]) for k in range(4)]
 
@@ -403,6 +430,10 @@
             for n in range(2):
                 sent(gathers[n])
         step(op, i, j)
+        if op == "attend" and i == 3:
+            pass_rows(1)
+        if op == "b" and i == 0 and j == 1:
+            pass_rows(2)
     sent(gathers[2])
     sent(gathers[3])
     for k in range(3):
@@ -441,6 +472,7 @@
             vmem((3, 4, 256, 256), bf16),
             vmem((3, 4, 256, 256), bf16),
             vmem((4, 256, 256), bf16),
+            vmem((4, 2, 16, 512), bf16),
             dma((6,)),
             dma,
             dma,
@@ -450,6 +482,8 @@
             dma((4, 2, 19)),
             dma((4, 2)),
             dma((4, 2)),
+            dma((4,)),
+            dma((4,)),
             dma((3, 4, 2)),
             dma((3, 4, 2)),
             dma((4,)),

time: 70.4 us -> 69.7 us (0.990)
    pallas_call x1, Pallas kernels: 68.3 us -> 67.6 us  [local(): pl.pallas_call(kernel, out_shape=jax.ShapeDtypeStruct((256, 1024), bf16),...]
where the time goes in v4:
time: 69.7 us; the launch traced here: 69.4 us
  Pallas kernels  67.6 us (97%)
  local copies, waits for them, and re-layouts  1.87 us (3%)
    pallas_call x1, Pallas kernels, local(): pl.pallas_call(kernel, out_shape=jax.ShapeDtypeStruct((256, 1024), bf16),...  67.6 us
    unnamed x1, local copies, waits for them, and re-layouts  1.87 us

profile of v4, /device:TPU:6, one launch (start us, length us, event | category | flops | bytes accessed | tf_op | source)
XLA Modules:
  0.0 69.4 jit_solution(5380563530433848732)
XLA Ops:
  0.0 67.6 %shard_map.64 = bf16[256,1024]{1,0:T(8,128)(2,1)} custom-call(s32[8]{0:T(128)} %lengths_in.1, s32[256]{0:T(256)} %units_in.1, bf16[128,1024]{1,0:T(8,128)(2,1)} %q_ref.1, bf16[2,64,128]{2,1,0:T(8,128)(2,1)} %bitcast.2, bf16[2,64,128]{2,1,0:T(8,128)(2,1)} %bitcast.3, bf16[1024,1024]{1,0:T(8,128)(2,1)} %w_ref.1), custom_call_target="tpu_custom_call" | custom-call | flops 5500000256 | bytes 8000000 | tf_op jit(solution)/shard_map/pallas_call | solution.py:452
  67.6 1.9 %copy.8 = bf16[256,1024]{1,0:T(8,128)(2,1)} copy(bf16[256,1024]{1,0:T(8,128)(2,1)} %shard_map.64) | data formatting | bytes 1048576
